TPU v7x, 32 devices: a whole 2x2x4 slice. The times are simulated.
32 devices in a mesh: parts: 2 (over x), blocks: 16 (over z, y, core).
Axes of the slice: x: 2, y: 2, z: 4, core: 2. Of those that a mesh axis runs over, the one named last changes fastest.
Arguments:
- coords: float32 [640, 3, 32768], P('blocks', None, 'parts'), parts along dimension 2
- pairs: int32 [2, 2048], replicated, may hold values from 0 to 639
- res_slot: int32 [640], replicated, may hold values from 0 to 639, each once
Outputs:
- distances: bfloat16 [4, 32768, 1024], P(None, ('parts', 'blocks')), parts along dimension 1
There are 2 independent parts, one for each index of `parts`. A program takes and returns all parts, laid end to end along the dimension named above; an argument that names none is the same for every part. Nothing has to cross between parts.
All inputs are finite; a program needn't handle non-finite values.
Results may differ from a plain program's by a relative error of at most 0.0025.
Values may be sent and summed in bfloat16 or wider, within the bound.
A program may use at most 192 MiB of HBM per device.

v0:
```python
import jax
import jax.numpy as jnp
from jax import lax
from jax.sharding import PartitionSpec as P

ROUNDS = 4


def shifted(shard, axis, by):
    count = lax.axis_size(axis)
    return lax.ppermute(shard, axis, [(i, (i + by) % count) for i in range(count)])


def row_norms(features):
    wide = features.astype(jnp.float32)
    return jnp.sum(wide * wide, axis=1)


def shards(coords, pairs, res_slot):
    width_blocks = lax.axis_size("blocks")
    res_local, _, frames = coords.shape
    per_block = frames // width_blocks
    residues = res_local * width_blocks
    position = (
        jnp.zeros((residues,), jnp.int32).at[res_slot].set(jnp.arange(residues, dtype=jnp.int32))
    )
    slot_first = position[pairs[0]]
    slot_second = position[pairs[1]]
    split_coords = coords.reshape(res_local, 3, width_blocks, per_block)
    gathered = lax.all_to_all(split_coords, "blocks", split_axis=2, concat_axis=0, tiled=True)
    squared = jnp.zeros((slot_first.shape[0], gathered.shape[3]), jnp.float32)
    for component in range(3):
        offset = gathered[slot_first, component, 0] - gathered[slot_second, component, 0]
        squared = squared + offset * offset
    separation = jnp.sqrt(squared + 0.01)
    features = jax.nn.sigmoid((8.0 - separation) / 1.5).T.astype(jnp.bfloat16)
    own_norms = row_norms(features)
    results = []
    visitor = features
    for offset_round in range(1, ROUNDS + 1):
        visitor = shifted(visitor, "blocks", 1)
        vis_norms = row_norms(visitor)
        intersection = lax.dot_general(
            features, visitor, (((1,), (1,)), ((), ())), preferred_element_type=jnp.float32
        )
        ratio = intersection / (own_norms[:, None] + vis_norms[None, :] - intersection + 1e-06)
        results.append((1.0 - ratio).astype(jnp.bfloat16))
    return jnp.stack(results)


def solution(mesh):
    in_specs = (P("blocks", None, "parts"), P(), P())
    out_specs = P(None, ("parts", "blocks"), None)
    return jax.shard_map(shards, mesh=mesh, in_specs=in_specs, out_specs=out_specs, check_vma=False)
```

profile of v0, /device:TPU:0, one launch (start us, length us, event | category | flops | bytes accessed | tf_op | source)
XLA Modules:
  0.0 669.2 jit_solution(15430760271793867332)
XLA Ops:
  0.0 8.0 %copy.15 = f32[3,5,16,8,1024]{4,3,1,0,2:T(8,128)} copy(f32[3,5,16,8,1024]{4,3,2,1,0:T(8,128)} %bitcast.54) | data formatting | bytes 15728640 | tf_op jit(solution)/shard_map/reshape | solution.py:29
  8.0 0.0 copy-start.2
  8.0 0.0 copy-start.1
  8.0 7.6 %all-to-all-start = ((f32[40,3,16,1024]{3,0,1,2:T(8,128)}), f32[40,3,16,1024]{3,0,1,2:T(8,128)}, u32[]{:S(2)}, u32[]{:S(2)}) async-start(f32[40,3,16,1024]{3,0,1,2:T(8,128)} %bitcast.53), calls=%async_computation | async-start | bytes 15728640 | tf_op jit(solution)/shard_map/all_to_all | solution.py:30
  15.6 0.0 copy-done.2
  15.6 4.3 scatter_custom_fusion
  19.9 0.0 copy-done.1
  19.9 8.6 %gather_fusion.2 = s32[2048]{0:T(1024)S(1)} fusion(s32[640]{0:T(1024)S(1)} %scatter_custom_fusion, s32[2048]{0:T(1024)S(1)} %broadcast_clamp_fusion), kind=kCustom, calls=%fused_computation.2 | custom fusion | bytes 24576 | tf_op jit(solution)/shard_map/gather | solution.py:28
  28.5 8.6 %gather_fusion = s32[2048]{0:T(1024)S(1)} fusion(s32[640]{0:T(1024)S(1)} %scatter_custom_fusion, s32[2048]{0:T(1024)S(1)} %broadcast_clamp_fusion.1), kind=kCustom, calls=%fused_computation | custom fusion | bytes 24576 | tf_op jit(solution)/shard_map/gather | solution.py:27
  37.2 119.9 %all-to-all-done = f32[40,3,16,1024]{3,0,1,2:T(8,128)} async-done(((f32[40,3,16,1024]{3,0,1,2:T(8,128)}), f32[40,3,16,1024]{3,0,1,2:T(8,128)}, u32[]{:S(2)}, u32[]{:S(2)}) %all-to-all-start) | async-done | bytes 7864352 | tf_op jit(solution)/shard_map/all_to_all | solution.py:30
  157.1 10.7 %copy.11 = f32[16,40,3,1,1024]{4,3,2,1,0:T(1,128)} copy(f32[16,40,3,1,1024]{4,1,2,0,3:T(8,128)} %bitcast.2) | data formatting | bytes 15728640 | tf_op jit(solution)/shard_map/all_to_all | solution.py:30
  167.8 39.1 %gather_fusion.7 = f32[2048,1024]{1,0:T(8,128)} fusion(f32[640,3,1,1024]{3,2,1,0:T(1,128)} %bitcast.41, s32[2048]{0:T(1024)S(1)} %bitcast.52), kind=kCustom, calls=%fused_computation.7 | custom fusion | bytes 16801792 | tf_op jit(solution)/shard_map/gather | solution.py:33
  206.9 38.8 %gather_fusion.6 = f32[2048,1024]{1,0:T(8,128)} fusion(f32[640,3,1,1024]{3,2,1,0:T(1,128)} %bitcast.42, s32[2048]{0:T(1024)S(1)} %bitcast.51), kind=kCustom, calls=%fused_computation.6 | custom fusion | bytes 16801792 | tf_op jit(solution)/shard_map/gather | solution.py:33
  245.7 39.0 %gather_fusion.5 = f32[2048,1024]{1,0:T(8,128)} fusion(f32[640,3,1,1024]{3,2,1,0:T(1,128)} %bitcast.43, s32[2048]{0:T(1024)S(1)} %bitcast.50), kind=kCustom, calls=%fused_computation.5 | custom fusion | bytes 16801792 | tf_op jit(solution)/shard_map/gather | solution.py:33
  284.8 39.1 %gather_fusion.4 = f32[2048,1024]{1,0:T(8,128)} fusion(f32[640,3,1,1024]{3,2,1,0:T(1,128)} %bitcast.44, s32[2048]{0:T(1024)S(1)} %bitcast.49), kind=kCustom, calls=%fused_computation.4 | custom fusion | bytes 16801792 | tf_op jit(solution)/shard_map/gather | solution.py:33
  323.8 38.9 %gather_fusion.3 = f32[2048,1024]{1,0:T(8,128)} fusion(f32[640,3,1,1024]{3,2,1,0:T(1,128)} %bitcast.45, s32[2048]{0:T(1024)S(1)} %bitcast.48), kind=kCustom, calls=%fused_computation.3 | custom fusion | bytes 16801792 | tf_op jit(solution)/shard_map/gather | solution.py:33
  362.7 39.0 %gather_fusion.1 = f32[2048,1024]{1,0:T(8,128)} fusion(f32[640,3,1,1024]{3,2,1,0:T(1,128)} %bitcast.46, s32[2048]{0:T(1024)S(1)} %bitcast.47), kind=kCustom, calls=%fused_computation.1 | custom fusion | bytes 16801792 | tf_op jit(solution)/shard_map/gather | solution.py:33
  401.7 21.2 %multiply_reduce_fusion.4 = (f32[1024]{0:T(1024)S(1)}, bf16[2048,1024]{1,0:T(8,128)(2,1)}) fusion(f32[2048,1024]{1,0:T(8,128)} %gather_fusion.6, f32[2048,1024]{1,0:T(8,128)} %gather_fusion.7, f32[2048,1024]{1,0:T(8,128)} %gather_fusion.4, f32[2048,1024]{1,0:T(8,128)} %gather_fusion.5, f32[2048,1024]{1,0:T(8,128)} %gather_fusion.1, f32[2048,1024]{1,0:T(8,128)} %gather_fusion.3), kind=kLoop, calls=%fused_computation.15 | loop fusion | flops 37747712 | bytes 54530048 | tf_op jit(solution)/shard_map/reduce_sum | solution.py:16
  422.9 0.0 copy-start
  422.9 0.8 collective-permute-start
  423.7 78.6 %collective-permute-done = bf16[1024,2048]{0,1:T(8,128)(2,1)S(1)} collective-permute-done((bf16[1024,2048]{0,1:T(8,128)(2,1)}, bf16[1024,2048]{0,1:T(8,128)(2,1)S(1)}, u32[]{:S(2)}, u32[]{:S(2)}) %collective-permute-start) | collective-permute-done | bytes 4194336 | tf_op jit(solution)/shard_map/ppermute | solution.py:11
  502.3 0.0 collective-permute-start.1
  502.3 50.6 %collective-permute-done.1 = bf16[1024,2048]{0,1:T(8,128)(2,1)S(1)} collective-permute-done((bf16[1024,2048]{0,1:T(8,128)(2,1)S(1)}, bf16[1024,2048]{0,1:T(8,128)(2,1)S(1)}, u32[]{:S(2)}, u32[]{:S(2)}) %collective-permute-start.1) | collective-permute-done | bytes 4194336 | tf_op jit(solution)/shard_map/ppermute | solution.py:11
  552.9 0.0 collective-permute-start.2
  552.9 50.6 %collective-permute-done.2 = bf16[1024,2048]{0,1:T(8,128)(2,1)S(1)} collective-permute-done((bf16[1024,2048]{0,1:T(8,128)(2,1)S(1)}, bf16[1024,2048]{0,1:T(8,128)(2,1)S(1)}, u32[]{:S(2)}, u32[]{:S(2)}) %collective-permute-start.2) | collective-permute-done | bytes 4194336 | tf_op jit(solution)/shard_map/ppermute | solution.py:11
  603.5 0.0 collective-permute-start.3
  603.5 0.9 multiply_reduce_fusion.3
  604.5 0.0 copy-done
  604.5 4.7 fusion.12
  609.2 0.9 multiply_reduce_fusion.2
  610.2 6.4 fusion.13
  616.6 0.9 multiply_reduce_fusion.1
  617.5 6.2 fusion.14
  623.7 30.5 %collective-permute-done.3 = bf16[1024,2048]{0,1:T(8,128)(2,1)S(1)} collective-permute-done((bf16[1024,2048]{0,1:T(8,128)(2,1)S(1)}, bf16[1024,2048]{0,1:T(8,128)(2,1)S(1)}, u32[]{:S(2)}, u32[]{:S(2)}) %collective-permute-start.3) | collective-permute-done | bytes 4194336 | tf_op jit(solution)/shard_map/ppermute | solution.py:11
  654.2 0.9 multiply_reduce_fusion
  655.1 10.2 %fusion = (bf16[1,1024,1024]{2,1,0:T(8,128)(2,1)S(1)}, bf16[1,1024,1024]{2,1,0:T(8,128)(2,1)S(1)}, bf16[1,1024,1024]{2,1,0:T(8,128)(2,1)S(1)}, bf16[1,1024,1024]{2,1,0:T(8,128)(2,1)S(1)}) fusion(f32[1024,1024]{1,0:T(8,128)S(1)} %fusion.12, f32[1024]{0:T(1024)S(1)} %multiply_reduce_fusion.3, f32[1024]{0:T(1024)S(1)} %get-tuple-element.5, ...), kind=kOutput, calls=%fused_computation.21 | convolution fusion | flops 4320133120 | bytes 29380608 | tf_op jit(solution)/shard_map/dot_general | solution.py:43
  665.3 3.9 pad_maximum_fusion
  (9 shorter events, 0.1 us)
Async XLA Ops:
  8.0 7.6 %copy-start.2 = (s32[640]{0:T(1024)S(1)}, s32[640]{0:T(1024)}, u32[]{:S(2)}) copy-start(s32[640]{0:T(1024)} %param.5) | copy-start | bytes 7684
  8.0 11.9 %copy-start.1 = (s32[2,2048]{1,0:T(2,128)S(1)}, s32[2,2048]{1,0:T(2,128)}, u32[]{:S(2)}) copy-start(s32[2,2048]{1,0:T(2,128)} %param.4) | copy-start | bytes 49156
  8.0 149.2 %all-to-all-start = ((f32[40,3,16,1024]{3,0,1,2:T(8,128)}), f32[40,3,16,1024]{3,0,1,2:T(8,128)}, u32[]{:S(2)}, u32[]{:S(2)}) async-start(f32[40,3,16,1024]{3,0,1,2:T(8,128)} %bitcast.53), calls=%async_computation | async-start | bytes 15728640 | tf_op jit(solution)/shard_map/all_to_all | solution.py:30
  422.9 181.6 %copy-start = (bf16[2048,1024]{1,0:T(8,128)(2,1)S(1)}, bf16[2048,1024]{1,0:T(8,128)(2,1)}, u32[]{:S(2)}) copy-start(bf16[2048,1024]{1,0:T(8,128)(2,1)} %get-tuple-element.6) | copy-start | bytes 12582916
  422.9 79.4 %collective-permute-start = (bf16[1024,2048]{0,1:T(8,128)(2,1)}, bf16[1024,2048]{0,1:T(8,128)(2,1)S(1)}, u32[]{:S(2)}, u32[]{:S(2)}) collective-permute-start(bf16[1024,2048]{0,1:T(8,128)(2,1)} %bitcast.55), channel_id=1, source_target_pairs={{0,1},{1,2},{2,3},{3,4},{4,5},{5,6},{6,7},{7,8},{8,9},{9,10},{10,1... | collective-permute-start | bytes 12582920 | tf_op jit(solution)/shard_map/ppermute | solution.py:11
  502.3 50.6 %collective-permute-start.1 = (bf16[1024,2048]{0,1:T(8,128)(2,1)S(1)}, bf16[1024,2048]{0,1:T(8,128)(2,1)S(1)}, u32[]{:S(2)}, u32[]{:S(2)}) collective-permute-start(bf16[1024,2048]{0,1:T(8,128)(2,1)S(1)} %collective-permute-done), channel_id=1, source_target_pairs={{0,1},{1,2},{2,3},{3,4},{4,5},{5,6},{6,7},{7,8},{8,9},{9,10},{10,1... | collective-permute-start | bytes 12582920 | tf_op jit(solution)/shard_map/ppermute | solution.py:11
  552.9 50.6 %collective-permute-start.2 = (bf16[1024,2048]{0,1:T(8,128)(2,1)S(1)}, bf16[1024,2048]{0,1:T(8,128)(2,1)S(1)}, u32[]{:S(2)}, u32[]{:S(2)}) collective-permute-start(bf16[1024,2048]{0,1:T(8,128)(2,1)S(1)} %collective-permute-done.1), channel_id=1, source_target_pairs={{0,1},{1,2},{2,3},{3,4},{4,5},{5,6},{6,7},{7,8},{8,9},{9,10},{10,1... | collective-permute-start | bytes 12582920 | tf_op jit(solution)/shard_map/ppermute | solution.py:11
  603.5 50.6 %collective-permute-start.3 = (bf16[1024,2048]{0,1:T(8,128)(2,1)S(1)}, bf16[1024,2048]{0,1:T(8,128)(2,1)S(1)}, u32[]{:S(2)}, u32[]{:S(2)}) collective-permute-start(bf16[1024,2048]{0,1:T(8,128)(2,1)S(1)} %collective-permute-done.2), channel_id=1, source_target_pairs={{0,1},{1,2},{2,3},{3,4},{4,5},{5,6},{6,7},{7,8},{8,9},{9,10},{10,1... | collective-permute-start | bytes 12582920 | tf_op jit(solution)/shard_map/ppermute | solution.py:11
where the time goes:
time: 673 us; the launch traced here: 669 us
  waiting for transfers between devices  330 us (49%)
  local copies, waits for them, and re-layouts  274 us (41%)
  other arithmetic  28.9 us (4%)
  matrix products  27.5 us (4%)
  starting transfers between devices  8.34 us (1%)
    ppermute x4, waiting for transfers between devices, shifted(): lax.ppermute(shard, axis, [(i, (i + by) % count) for i in range(count)])  210 us
    all_to_all x1, waiting for transfers between devices, shards(): lax.all_to_all(split_coords, 'blocks', split_axis=2, concat_axis=0, tiled...  120 us
    gather x3, local copies, waits for them, and re-layouts, shards(): gathered[slot_second, component, 0]  117 us
    gather x3, local copies, waits for them, and re-layouts, shards(): gathered[slot_first, component, 0] - gathered[slot_second, component, 0]  117 us
    dot_general x4, matrix products, shards(): lax.dot_general(features, visitor, (((1,), (1,)), ((), ())), preferred_el...  27.5 us
    reduce_sum x5, other arithmetic, row_norms(): return jnp.sum(wide * wide, axis=1)  24.9 us
  transfers between devices with their start and end apart: 5, of which 5 were waited for; matrix products, arithmetic and copies ran while one was open for 6% of the time, Pallas kernels for 0%

commit v1 on v0

v1 whole, which is shorter than its diff:
```python
import functools
import jax
import jax.numpy as jnp
from jax import lax
from jax.experimental import pallas as pl
from jax.experimental.pallas import tpu as pltpu
from jax.sharding import PartitionSpec as P

ROUNDS = 4
LANES = 128
TOP_CODE = 32767.0
MESH = pl.DeviceIdType.MESH


def encode_kernel(x_ref, code_ref, meta_ref, tmp, params):
    _, res, frames = x_ref.shape
    rows = frames // LANES
    half = None
    centers = []
    for k in range(3):
        x = x_ref[k]
        top = jnp.max(x, axis=0, keepdims=True)
        low = jnp.min(x, axis=0, keepdims=True)
        center = (0.5 * top + 0.5 * low).astype(jnp.bfloat16).astype(jnp.float32)
        reach = jnp.maximum(top - center, center - low)
        half = reach if half is None else jnp.maximum(half, reach)
        centers.append(center)
    step = jnp.maximum(half * (1.01 / TOP_CODE), 1e-30).astype(jnp.bfloat16).astype(jnp.float32)
    inverse = 1.0 / step
    for k in range(3):
        scaled = jnp.round((x_ref[k] - centers[k]) * inverse)
        for s in range(rows):
            tmp[pl.ds(s, res, stride=rows), :] = scaled[:, s * LANES:(s + 1) * LANES]
        code_ref[0, k] = tmp[...].astype(jnp.int32).astype(jnp.int16)
    for k, plane in enumerate(centers + [step]):
        for s in range(rows):
            params[k * rows + s:k * rows + s + 1, :] = plane[:, s * LANES:(s + 1) * LANES]
    meta_ref[0] = params[...].astype(jnp.bfloat16)


def encode(coords, blocks):
    _, res, frames = coords.shape
    per_block = frames // blocks
    rows = per_block // LANES
    return pl.pallas_call(
        encode_kernel,
        grid=(blocks,),
        in_specs=[pl.BlockSpec((3, res, per_block), lambda d: (0, 0, d))],
        out_specs=[
            pl.BlockSpec((1, 3, res * rows, LANES), lambda d: (d, 0, 0, 0)),
            pl.BlockSpec((1, 4 * rows, LANES), lambda d: (d, 0, 0)),
        ],
        out_shape=[
            jax.ShapeDtypeStruct((blocks, 3, res * rows, LANES), jnp.int16),
            jax.ShapeDtypeStruct((blocks, 4 * rows, LANES), jnp.bfloat16),
        ],
        scratch_shapes=[
            pltpu.VMEM((res * rows, LANES), jnp.float32),
            pltpu.VMEM((4 * rows, LANES), jnp.float32),
        ],
        compiler_params=pltpu.CompilerParams(vmem_limit_bytes=32 * 2**20),
    )(coords)


def feature_kernel(first_ref, second_ref, code_ref, meta_ref, out_ref, grid_ref, tmp):
    blocks, _, span, _ = code_ref.shape
    rows = meta_ref.shape[1] // 4
    contacts = out_ref.shape[0]

    def decode(b, carry):
        meta = meta_ref[b].astype(jnp.float32)
        step = meta[3 * rows:4 * rows][None]
        for k in range(3):
            code = code_ref[b, k].astype(jnp.int32).astype(jnp.float32)
            value = code.reshape(span // rows, rows, LANES) * step + meta[k * rows:(k + 1) * rows][None]
            grid_ref[k, pl.ds(b * (span // rows), span // rows)] = value
        return carry

    lax.fori_loop(0, blocks, decode, 0)
    group = 16

    def contact_group(i, carry):
        start = pl.multiple_of(i * group, group)
        for j in range(group):
            a = first_ref[start + j]
            b = second_ref[start + j]
            squared = None
            for k in range(3):
                offset = grid_ref[k, a] - grid_ref[k, b]
                term = offset * offset
                squared = term if squared is None else squared + term
            separation = jnp.sqrt(squared + 0.01)
            tmp[pl.ds(j, rows, stride=group), :] = 1.0 / (1.0 + jnp.exp((separation - 8.0) / 1.5))
        for s in range(rows):
            out_ref[pl.ds(start, group), s * LANES:(s + 1) * LANES] = (
                tmp[s * group:(s + 1) * group, :].astype(jnp.bfloat16)
            )
        return carry

    lax.fori_loop(0, contacts // group, contact_group, 0)


def featurize(first, second, codes, meta):
    blocks, _, span, _ = codes.shape
    rows = meta.shape[1] // 4
    contacts = first.shape[0]
    residues = blocks * span // rows
    whole = pl.BlockSpec(memory_space=pltpu.VMEM)
    scalars = pl.BlockSpec(memory_space=pltpu.SMEM)
    return pl.pallas_call(
        feature_kernel,
        in_specs=[scalars, scalars, whole, whole],
        out_specs=whole,
        out_shape=jax.ShapeDtypeStruct((contacts, rows * LANES), jnp.bfloat16),
        scratch_shapes=[
            pltpu.VMEM((3, residues, rows, LANES), jnp.float32),
            pltpu.VMEM((rows * 16, LANES), jnp.float32),
        ],
        compiler_params=pltpu.CompilerParams(vmem_limit_bytes=48 * 2**20),
    )(first, second, codes, meta)


PREV, SIDE, NEAR, FAR = range(4)


def exchange_kernel(blocks, chunks, own_ref, out_ref, own_t, visit, total, norms, own_norm, stage,
                    send_sem, recv_sem, out_sem):
    me = lax.axis_index("blocks")
    core = me % 2
    side = (me // 2) % 2
    ahead = (me + 4) % blocks
    behind = (me + blocks - 4) % blocks
    twin = me + 1 - 2 * core
    across = me + 2 - 4 * side
    contacts, frames = own_ref.shape
    depth = contacts // chunks

    barrier = pltpu.get_barrier_semaphore()
    for other in (ahead, behind, twin, across):
        pl.semaphore_signal(barrier, inc=1, device_id={"blocks": other}, device_id_type=MESH)
    pl.semaphore_wait(barrier, 4)

    def part(n):
        return pl.ds(pl.multiple_of(n * depth, depth), depth)

    def copy(stream, n, source, target):
        return pltpu.make_async_remote_copy(
            src_ref=source.at[part(n)],
            dst_ref=visit.at[stream, part(n)],
            send_sem=send_sem.at[stream, n],
            recv_sem=recv_sem.at[stream, n],
            device_id={"blocks": target},
            device_id_type=MESH,
        )

    prev = visit.at[PREV]

    def first_sends(n, carry):
        copy(PREV, n, own_ref, ahead).start()

        @pl.when(side == 0)
        def _():
            copy(SIDE, n, own_ref, across).start()

        @pl.when(core == 0)
        def _():
            copy(NEAR, n, own_ref, twin).start()

        return carry

    lax.fori_loop(0, chunks, first_sends, 0)

    norms[...] = jnp.zeros_like(norms)

    def turn(n, own):
        block = own_ref[part(n), :]
        own_t[n] = block.T
        wide = block.astype(jnp.float32)
        return own + jnp.sum(wide * wide, axis=0, keepdims=True)

    own = lax.fori_loop(0, chunks, turn, jnp.zeros((1, frames), jnp.float32))
    own_norm[...] = jnp.broadcast_to(own, (LANES, frames)).T

    tile = 256

    def add(stream, n):
        block = visit[stream, part(n), :]
        wide = block.astype(jnp.float32)
        norms[stream] += jnp.sum((wide * wide).reshape(depth // 8, 8, frames), axis=0)

        def rows_of(t, carry):
            at = pl.ds(pl.multiple_of(t * tile, tile), tile)
            product = jnp.dot(own_t[n, at, :], block_of(stream, n), preferred_element_type=jnp.float32)

            @pl.when(n == 0)
            def _():
                total[stream, at, :] = product

            @pl.when(n > 0)
            def _():
                total[stream, at, :] += product

            return carry

        lax.fori_loop(0, frames // tile, rows_of, 0)

    def block_of(stream, n):
        return visit[stream, part(n), :]

    def arrive(n, carry):
        @pl.when(n < chunks)
        def _():
            copy(PREV, n, own_ref, ahead).wait_recv()

            @pl.when(side == 1)
            def _():
                copy(SIDE, n, prev, across).start()

            @pl.when(core == 1)
            def _():
                copy(NEAR, n, prev, twin).start()

        @pl.when(n > 0)
        def _():
            copy(SIDE, n - 1, prev, across).wait_recv()
            copy(FAR, n - 1, visit.at[SIDE], twin).start()

        @pl.when(n < chunks)
        def _():
            add(PREV, n)

        @pl.when(n > 0)
        def _():
            copy(NEAR, n - 1, prev, twin).wait_recv()
            add(NEAR, n - 1)
            add(SIDE, n - 1)
            copy(FAR, n - 1, prev, twin).wait_recv()
            add(FAR, n - 1)

        return carry

    lax.fori_loop(0, chunks + 1, arrive, 0)

    def out_copy(stream, round_index):
        return pltpu.make_async_copy(stage.at[stream], out_ref.at[round_index], out_sem.at[stream])

    round_of = {PREV: 3, SIDE: 1, NEAR: 2 - 2 * core, FAR: 2 * core}
    for stream in (PREV, NEAR, SIDE, FAR):
        visiting = jnp.sum(norms[stream], axis=0, keepdims=True)

        def finish(t, carry):
            at = pl.ds(pl.multiple_of(t * tile, tile), tile)
            shared = total[stream, at, :]
            ratio = shared / (own_norm[at, :1] + visiting - shared + 1e-06)
            stage[stream, at, :] = (1.0 - ratio).astype(jnp.bfloat16)
            return carry

        lax.fori_loop(0, frames // tile, finish, 0)
        out_copy(stream, round_of[stream]).start()

    def drain(n, carry):
        for stream in range(4):
            copy(stream, n, prev, twin).wait_send()
        return carry

    lax.fori_loop(0, chunks, drain, 0)
    for stream in (PREV, NEAR, SIDE, FAR):
        out_copy(stream, round_of[stream]).wait()


def exchange(features, blocks):
    contacts, frames = features.shape
    chunks = 8
    depth = contacts // chunks
    return pl.pallas_call(
        functools.partial(exchange_kernel, blocks, chunks),
        in_specs=[pl.BlockSpec(memory_space=pltpu.VMEM)],
        out_specs=pl.BlockSpec(memory_space=pl.ANY),
        out_shape=jax.ShapeDtypeStruct((ROUNDS, frames, frames), jnp.bfloat16),
        scratch_shapes=[
            pltpu.VMEM((chunks, frames, depth), jnp.bfloat16),
            pltpu.VMEM((4, contacts, frames), jnp.bfloat16),
            pltpu.VMEM((4, frames, frames), jnp.float32),
            pltpu.VMEM((4, 8, frames), jnp.float32),
            pltpu.VMEM((frames, LANES), jnp.float32),
            pltpu.VMEM((4, frames, frames), jnp.bfloat16),
            pltpu.SemaphoreType.DMA((4, chunks)),
            pltpu.SemaphoreType.DMA((4, chunks)),
            pltpu.SemaphoreType.DMA((4,)),
        ],
        compiler_params=pltpu.CompilerParams(
            collective_id=1, has_side_effects=True, vmem_limit_bytes=60 * 2**20
        ),
    )(features)


def shards(coords, pairs, res_slot):
    blocks = lax.axis_size("blocks")
    residues = coords.shape[0] * blocks
    position = (
        jnp.zeros((residues,), jnp.int32).at[res_slot].set(jnp.arange(residues, dtype=jnp.int32))
    )
    codes, meta = encode(coords.transpose(1, 0, 2), blocks)
    codes = lax.all_to_all(codes, "blocks", 0, 0, tiled=True)
    meta = lax.all_to_all(meta, "blocks", 0, 0, tiled=True)
    features = featurize(position[pairs[0]], position[pairs[1]], codes, meta)
    return exchange(features, blocks)


def solution(mesh):
    in_specs = (P("blocks", None, "parts"), P(), P())
    out_specs = P(None, ("parts", "blocks"), None)
    return jax.shard_map(shards, mesh=mesh, in_specs=in_specs, out_specs=out_specs, check_vma=False)
```

time: 673 us -> 262 us (0.39)
  waiting for transfers between devices: 330 us -> 51.7 us
  local copies, waits for them, and re-layouts: 274 us -> 34.2 us
  Pallas kernels: 0 us -> 156 us
  other arithmetic: 28.9 us -> 0.04 us
  matrix products: 27.5 us -> 0 us
  blocking collectives: 0 us -> 15.1 us
    gather x8 -> x2, local copies, waits for them, and re-layouts: 251 us -> 17.2 us  [shards(): features = featurize(position[pairs[0]], position[pairs[1]], codes, meta)]
    ppermute x4 -> x0, waiting for transfers between devices: 210 us -> none  [shifted(): lax.ppermute(shard, axis, [(i, (i + by) % count) for i in range(count)])]
    pallas_call x0 -> x3, Pallas kernels: none -> 156 us  [the longest x1 135 us: exchange(): pl.pallas_call(functools.partial(exchange_kernel, blocks, chunks), in_spe...]
    all_to_all x1, waiting for transfers between devices: 120 us -> 51.7 us  [shards(): codes = lax.all_to_all(codes, 'blocks', 0, 0, tiled=True)]
    dot_general x4 -> x0, matrix products: 27.5 us -> none  [shards(): lax.dot_general(features, visitor, (((1,), (1,)), ((), ())), preferred_el...]
    reduce_sum x5 -> x0, other arithmetic: 24.9 us -> none  [row_norms(): return jnp.sum(wide * wide, axis=1)]
    all_to_all x0 -> x1, blocking collectives: none -> 15.1 us  [shards(): meta = lax.all_to_all(meta, 'blocks', 0, 0, tiled=True)]
    unnamed x6 -> x9, local copies, waits for them, and re-layouts: 0.01 us -> 12.9 us
  transfers between devices with their start and end apart: 5 -> 1, of which waited for: 5 -> 1; matrix products, arithmetic and copies ran while one was open for 6% -> 8% of each run, Pallas kernels for 0% -> 0%
where the time goes in v1:
time: 262 us
  Pallas kernels  156 us (60%)
  waiting for transfers between devices  51.7 us (20%)
  local copies, waits for them, and re-layouts  34.2 us (13%)
  blocking collectives  15.1 us (6%)
  starting transfers between devices  4.52 us (2%)
    pallas_call x1, Pallas kernels, exchange(): pl.pallas_call(functools.partial(exchange_kernel, blocks, chunks), in_spe...  135 us
    all_to_all x1, waiting for transfers between devices, shards(): codes = lax.all_to_all(codes, 'blocks', 0, 0, tiled=True)  51.7 us
    gather x2, local copies, waits for them, and re-layouts, shards(): features = featurize(position[pairs[0]], position[pairs[1]], codes, meta)  17.2 us
    pallas_call x1, Pallas kernels, featurize(): pl.pallas_call(feature_kernel, in_specs=[scalars, scalars, whole, whole],...  16.7 us
    all_to_all x1, blocking collectives, shards(): meta = lax.all_to_all(meta, 'blocks', 0, 0, tiled=True)  15.1 us
    unnamed x9, local copies, waits for them, and re-layouts  12.9 us
  transfers between devices with their start and end apart: 1, of which 1 were waited for; matrix products, arithmetic and copies ran while one was open for 8% of the time, Pallas kernels for 0%

profile of v1, /device:TPU:0, one launch (start us, length us, event | category | flops | bytes accessed | tf_op | source)
XLA Modules:
  0.0 261.8 jit_solution(15055523738781858340)
XLA Ops:
  0.0 0.0 copy-start
  0.0 3.2 %copy-done = f32[40,3,16384]{2,0,1:T(8,128)S(1)} copy-done((f32[40,3,16384]{2,0,1:T(8,128)S(1)}, f32[40,3,16384]{2,0,1:T(8,128)}, u32[]{:S(2)}) %copy-start) | copy-done | bytes 7864344
  3.2 0.0 copy-start.3
  3.2 0.0 copy-start.2
  3.2 4.9 %shard_map.37 = (s16[16,3,320,128]{3,2,1,0:T(8,128)(2,1)S(1)}, bf16[16,32,128]{2,1,0:T(8,128)(2,1)S(1)}) custom-call(f32[3,40,16384]{2,1,0:T(8,128)S(1)} %bitcast.8), custom_call_target="tpu_custom_call" | custom-call | tf_op jit(solution)/shard_map/pallas_call | solution.py:45
  8.2 0.0 copy-start.1
  8.2 1.9 copy-done.1
  10.1 15.1 %all_to_all.10.meta_ref = bf16[16,32,128]{2,1,0:T(8,128)(2,1)S(1)} all-to-all(bf16[16,32,128]{2,1,0:T(8,128)(2,1)S(1)} %get-tuple-element.8), channel_id=1, replica_groups=mesh['parts'=2,'blocks'=16] {'blocks'}, dimensions={0} | all-to-all | bytes 262144 | tf_op jit(solution)/shard_map/all_to_all | solution.py:305
  25.2 4.5 %all-to-all-start = ((s16[16,3,320,128]{3,2,1,0:T(8,128)(2,1)}), s16[16,3,320,128]{3,2,1,0:T(8,128)(2,1)}, u32[]{:S(2)}, u32[]{:S(2)}) async-start(s16[16,3,320,128]{3,2,1,0:T(8,128)(2,1)} %copy-done.1), calls=%async_computation | async-start | bytes 7864320 | tf_op jit(solution)/shard_map/all_to_all | solution.py:304
  29.8 0.0 copy-done.3
  29.8 4.1 %scatter_custom_fusion = s32[640]{0:T(1024)S(1)} fusion(s32[640]{0:T(1024)S(1)} %compare_select_fusion.2, s32[640]{0:T(1024)S(1)} %iota.3, s32[]{:T(128)} %constant.2.clone.1), kind=kCustom, calls=%fused_computation.8 | custom fusion | bytes 2564 | tf_op jit(solution)/shard_map/scatter | solution.py:301
  33.9 0.0 copy-done.2
  33.9 8.6 %gather_fusion.1 = s32[2048]{0:T(1024)S(1)} fusion(s32[640]{0:T(1024)S(1)} %scatter_custom_fusion, s32[2048]{0:T(1024)S(1)} %broadcast_clamp_fusion), kind=kCustom, calls=%fused_computation.1 | custom fusion | bytes 24576 | tf_op jit(solution)/shard_map/gather | solution.py:306
  42.5 8.6 %gather_fusion = s32[2048]{0:T(1024)S(1)} fusion(s32[640]{0:T(1024)S(1)} %scatter_custom_fusion, s32[2048]{0:T(1024)S(1)} %broadcast_clamp_fusion.1), kind=kCustom, calls=%fused_computation | custom fusion | bytes 24576 | tf_op jit(solution)/shard_map/gather | solution.py:306
  51.1 51.7 %all-to-all-done.code_ref = s16[16,3,320,128]{3,2,1,0:T(8,128)(2,1)} async-done(((s16[16,3,320,128]{3,2,1,0:T(8,128)(2,1)}), s16[16,3,320,128]{3,2,1,0:T(8,128)(2,1)}, u32[]{:S(2)}, u32[]{:S(2)}) %all-to-all-start) | async-done | bytes 3932192 | tf_op jit(solution)/shard_map/all_to_all | solution.py:304
  102.8 16.7 %shard_map.38.own_ref = bf16[2048,1024]{1,0:T(8,128)(2,1)} custom-call(s32[2048]{0:T(1024)S(1)} %gather_fusion, s32[2048]{0:T(1024)S(1)} %gather_fusion.1, s16[16,3,320,128]{3,2,1,0:T(8,128)(2,1)} %all-to-all-done.code_ref, bf16[16,32,128]{2,1,0:T(8,128)(2,1)S(1)} %all_to_all.10.meta_ref), custom_call_target="tpu_custom_call" | custom-call | tf_op jit(solution)/shard_map/pallas_call | solution.py:110
  119.5 134.5 %shard_map.39 = bf16[4,1024,1024]{2,1,0:T(8,128)(2,1)} custom-call(bf16[2048,1024]{1,0:T(8,128)(2,1)} %shard_map.38.own_ref), custom_call_target="tpu_custom_call" | custom-call | tf_op jit(solution)/shard_map/pallas_call | solution.py:275
  254.0 7.8 %copy.5 = bf16[4,1024,1024]{2,1,0:T(8,128)(2,1)} copy(bf16[4,1024,1024]{2,1,0:T(8,128)(2,1)} %shard_map.39) | data formatting | bytes 16777216
  (5 shorter events, 0.0 us)
Async XLA Ops:
  0.0 3.2 %copy-start = (f32[40,3,16384]{2,0,1:T(8,128)S(1)}, f32[40,3,16384]{2,0,1:T(8,128)}, u32[]{:S(2)}) copy-start(f32[40,3,16384]{2,0,1:T(8,128)} %param.3) | copy-start | bytes 23592964
  3.2 26.5 %copy-start.3 = (s32[640]{0:T(1024)S(1)}, s32[640]{0:T(1024)}, u32[]{:S(2)}) copy-start(s32[640]{0:T(1024)} %param.5) | copy-start | bytes 7684
  3.2 30.7 %copy-start.2 = (s32[2,2048]{1,0:T(2,128)S(1)}, s32[2,2048]{1,0:T(2,128)}, u32[]{:S(2)}) copy-start(s32[2,2048]{1,0:T(2,128)} %param.4) | copy-start | bytes 49156
  8.2 1.9 copy-start.1
  25.2 77.6 %all-to-all-start = ((s16[16,3,320,128]{3,2,1,0:T(8,128)(2,1)}), s16[16,3,320,128]{3,2,1,0:T(8,128)(2,1)}, u32[]{:S(2)}, u32[]{:S(2)}) async-start(s16[16,3,320,128]{3,2,1,0:T(8,128)(2,1)} %copy-done.1), calls=%async_computation | async-start | bytes 7864320 | tf_op jit(solution)/shard_map/all_to_all | solution.py:304

commit v2 on v1

v2 whole, which is shorter than its diff:
```python
import functools
import math
import jax
import jax.numpy as jnp
from jax import lax
from jax.experimental import pallas as pl
from jax.experimental.pallas import tpu as pltpu
from jax.sharding import PartitionSpec as P

ROUNDS = 4
LANES = 128
TOP_CODE = 32000.0
COARSE = 256.0
LOG_TWO = math.log(2.0)
MESH = pl.DeviceIdType.MESH


def step_of(exponent):
    return jnp.exp(exponent * LOG_TWO)


def encode_kernel(x_ref, code_ref, tmp, params):
    _, res, frames = x_ref.shape
    rows = frames // LANES
    centers = []
    finest = jnp.full((1, frames), 1e-30, jnp.float32)
    for k in range(3):
        x = x_ref[k]
        top = jnp.max(x, axis=0, keepdims=True)
        low = jnp.min(x, axis=0, keepdims=True)
        center = 0.5 * top + 0.5 * low
        reach = jnp.maximum(top - center, center - low)
        finest = jnp.maximum(finest, jnp.maximum(reach, jnp.abs(center) * (1.0 / COARSE)) * (1.0 / TOP_CODE))
        centers.append(center)
    exponent = jnp.ceil(jnp.log(finest) * (1.0 / LOG_TWO))
    step = step_of(exponent)
    inverse = 1.0 / step
    planes = []
    for k in range(3):
        center_code = jnp.round(centers[k] * (1.0 / COARSE) * inverse)
        planes.append(center_code)
        scaled = jnp.round((x_ref[k] - center_code * (COARSE * step)) * inverse)
        for s in range(rows):
            tmp[pl.ds(s, res, stride=rows), :] = scaled[:, s * LANES:(s + 1) * LANES]
        code_ref[0, k * res * rows:(k + 1) * res * rows] = tmp[...].astype(jnp.int32).astype(jnp.int16)
    for k, plane in enumerate(planes + [exponent]):
        for s in range(rows):
            params[k * rows + s:k * rows + s + 1, :] = plane[:, s * LANES:(s + 1) * LANES]
    code_ref[0, 3 * res * rows:] = params[...].astype(jnp.int32).astype(jnp.int16)


def encode(coords, blocks):
    _, res, frames = coords.shape
    per_block = frames // blocks
    rows = per_block // LANES
    span = (3 * res + 4) * rows
    return pl.pallas_call(
        encode_kernel,
        grid=(blocks,),
        in_specs=[pl.BlockSpec((3, res, per_block), lambda d: (0, 0, d))],
        out_specs=pl.BlockSpec((1, span, LANES), lambda d: (d, 0, 0)),
        out_shape=jax.ShapeDtypeStruct((blocks, span, LANES), jnp.int16),
        scratch_shapes=[
            pltpu.VMEM((res * rows, LANES), jnp.float32),
            pltpu.VMEM((4 * rows, LANES), jnp.float32),
        ],
        compiler_params=pltpu.CompilerParams(vmem_limit_bytes=32 * 2**20),
    )(coords)


PREV, SIDE, NEAR, FAR = range(4)


def exchange_kernel(blocks, chunks, first_ref, second_ref, code_ref, out_ref, grid_ref, tmp, own_ref,
                    own_t, visit, total, norms, own_norm, stage, send_sem, recv_sem, out_sem):
    me = lax.axis_index("blocks")
    core = me % 2
    side = (me // 2) % 2
    ahead = (me + 4) % blocks
    behind = (me + blocks - 4) % blocks
    twin = me + 1 - 2 * core
    across = me + 2 - 4 * side
    contacts, frames = own_ref.shape
    rows = frames // LANES
    res = grid_ref.shape[1] // blocks
    depth = contacts // chunks
    wide_depth = 2 * depth

    barrier = pltpu.get_barrier_semaphore()
    for other in (ahead, behind, twin, across):
        pl.semaphore_signal(barrier, inc=1, device_id={"blocks": other}, device_id_type=MESH)

    def decode(b, carry):
        def numbers(start, count):
            return code_ref[b, start:start + count].astype(jnp.int32).astype(jnp.float32)

        params = numbers(3 * res * rows, 4 * rows)
        step = step_of(params[3 * rows:])
        for k in range(3):
            center = params[k * rows:(k + 1) * rows] * (COARSE * step)
            code = numbers(k * res * rows, res * rows).reshape(res, rows, LANES)
            grid_ref[k, pl.ds(b * res, res)] = code * step[None] + center[None]
        return carry

    lax.fori_loop(0, blocks, decode, 0)
    pl.semaphore_wait(barrier, 4)

    def part(n):
        return pl.ds(pl.multiple_of(n * depth, depth), depth)

    def pair(m):
        return pl.ds(pl.multiple_of(m * wide_depth, wide_depth), wide_depth)

    def copy(stream, n, source, target):
        return pltpu.make_async_remote_copy(
            src_ref=source.at[part(n)],
            dst_ref=visit.at[stream, part(n)],
            send_sem=send_sem.at[stream, n],
            recv_sem=recv_sem.at[stream, n],
            device_id={"blocks": target},
            device_id_type=MESH,
        )

    prev = visit.at[PREV]
    group = 16

    def features(n, carry):
        def contact_group(i, inner):
            start = pl.multiple_of(n * depth + i * group, group)
            for j in range(group):
                a = first_ref[start + j]
                b = second_ref[start + j]
                squared = None
                for k in range(3):
                    offset = grid_ref[k, a] - grid_ref[k, b]
                    term = offset * offset
                    squared = term if squared is None else squared + term
                separation = jnp.sqrt(squared + 0.01)
                tmp[pl.ds(j, rows, stride=group), :] = 1.0 / (1.0 + jnp.exp((separation - 8.0) / 1.5))
            for s in range(rows):
                own_ref[pl.ds(start, group), s * LANES:(s + 1) * LANES] = (
                    tmp[s * group:(s + 1) * group, :].astype(jnp.bfloat16)
                )
            return inner

        lax.fori_loop(0, depth // group, contact_group, 0)
        copy(PREV, n, own_ref, ahead).start()

        @pl.when(side == 0)
        def _():
            copy(SIDE, n, own_ref, across).start()

        @pl.when(core == 0)
        def _():
            copy(NEAR, n, own_ref, twin).start()

        return carry

    lax.fori_loop(0, chunks, features, 0)
    norms[...] = jnp.zeros_like(norms)
    tile = 256

    def squares(block):
        wide = block.astype(jnp.float32)
        return jnp.sum((wide * wide).reshape(wide_depth // 8, 8, frames), axis=0)

    def turn(m):
        block = own_ref[pair(m), :]
        own_t[m] = block.T
        norms[4] += squares(block)

    def add(stream, m):
        norms[stream] += squares(visit[stream, pair(m), :])

        def rows_of(t, carry):
            at = pl.ds(pl.multiple_of(t * tile, tile), tile)
            product = jnp.dot(
                own_t[m, at, :], visit[stream, pair(m), :], preferred_element_type=jnp.float32
            )

            @pl.when(m == 0)
            def _():
                total[stream, at, :] = product

            @pl.when(m > 0)
            def _():
                total[stream, at, :] += product

            return carry

        lax.fori_loop(0, frames // tile, rows_of, 0)

    def pass_far(n):
        copy(SIDE, n, prev, across).wait_recv()
        copy(FAR, n, visit.at[SIDE], twin).start()

    def arrive(n, carry):
        copy(PREV, n, own_ref, ahead).wait_recv()

        @pl.when(side == 1)
        def _():
            copy(SIDE, n, prev, across).start()

        @pl.when(core == 1)
        def _():
            copy(NEAR, n, prev, twin).start()

        @pl.when(n > 0)
        def _():
            pass_far(n - 1)

        m = n // 2

        @pl.when(n % 2 == 1)
        def _():
            turn(m)
            add(PREV, m)
            copy(NEAR, n - 1, prev, twin).wait_recv()
            copy(NEAR, n, prev, twin).wait_recv()
            add(NEAR, m)

        @pl.when((n % 2 == 0) & (n > 0))
        def _():
            add(SIDE, m - 1)
            copy(FAR, n - 2, prev, twin).wait_recv()
            copy(FAR, n - 1, prev, twin).wait_recv()
            add(FAR, m - 1)

        return carry

    lax.fori_loop(0, chunks, arrive, 0)

    slot_of = {PREV: 0, NEAR: 1, SIDE: 0, FAR: 1}
    round_of = {PREV: 3, SIDE: 1, NEAR: 2 - 2 * core, FAR: 2 * core}

    def out_copy(stream):
        return pltpu.make_async_copy(
            stage.at[slot_of[stream]], out_ref.at[round_of[stream]], out_sem.at[stream]
        )

    def finish(stream):
        visiting = jnp.sum(norms[stream], axis=0, keepdims=True)

        def rows_of(t, carry):
            at = pl.ds(pl.multiple_of(t * tile, tile), tile)
            shared = total[stream, at, :]
            ratio = shared / (own_norm[at, :1] + visiting - shared + 1e-06)
            stage[slot_of[stream], at, :] = (1.0 - ratio).astype(jnp.bfloat16)
            return carry

        lax.fori_loop(0, frames // tile, rows_of, 0)
        out_copy(stream).start()

    last = chunks // 2 - 1
    own = jnp.sum(norms[4], axis=0, keepdims=True)
    own_norm[...] = jnp.broadcast_to(own, (LANES, frames)).T
    finish(PREV)
    pass_far(chunks - 1)
    finish(NEAR)
    add(SIDE, last)
    out_copy(PREV).wait()
    finish(SIDE)
    copy(FAR, chunks - 2, prev, twin).wait_recv()
    copy(FAR, chunks - 1, prev, twin).wait_recv()
    add(FAR, last)
    out_copy(NEAR).wait()
    finish(FAR)

    def drain(n, carry):
        for stream in range(4):
            copy(stream, n, prev, twin).wait_send()
        return carry

    lax.fori_loop(0, chunks, drain, 0)
    out_copy(SIDE).wait()
    out_copy(FAR).wait()


def exchange(first, second, codes, residues):
    blocks, span, _ = codes.shape
    contacts = first.shape[0]
    rows = span // (3 * (residues // blocks) + 4)
    frames = rows * LANES
    chunks = 16
    depth = contacts // chunks
    scalars = pl.BlockSpec(memory_space=pltpu.SMEM)
    return pl.pallas_call(
        functools.partial(exchange_kernel, blocks, chunks),
        in_specs=[scalars, scalars, pl.BlockSpec(memory_space=pltpu.VMEM)],
        out_specs=pl.BlockSpec(memory_space=pl.ANY),
        out_shape=jax.ShapeDtypeStruct((ROUNDS, frames, frames), jnp.bfloat16),
        scratch_shapes=[
            pltpu.VMEM((3, residues, rows, LANES), jnp.float32),
            pltpu.VMEM((rows * 16, LANES), jnp.float32),
            pltpu.VMEM((contacts, frames), jnp.bfloat16),
            pltpu.VMEM((chunks // 2, frames, 2 * depth), jnp.bfloat16),
            pltpu.VMEM((4, contacts, frames), jnp.bfloat16),
            pltpu.VMEM((4, frames, frames), jnp.float32),
            pltpu.VMEM((5, 8, frames), jnp.float32),
            pltpu.VMEM((frames, LANES), jnp.float32),
            pltpu.VMEM((2, frames, frames), jnp.bfloat16),
            pltpu.SemaphoreType.DMA((4, chunks)),
            pltpu.SemaphoreType.DMA((4, chunks)),
            pltpu.SemaphoreType.DMA((4,)),
        ],
        compiler_params=pltpu.CompilerParams(
            collective_id=1, has_side_effects=True, vmem_limit_bytes=60 * 2**20
        ),
    )(first, second, codes)


def shards(coords, pairs, res_slot):
    blocks = lax.axis_size("blocks")
    residues = coords.shape[0] * blocks
    position = (
        jnp.zeros((residues,), jnp.int32).at[res_slot].set(jnp.arange(residues, dtype=jnp.int32))
    )
    codes = encode(coords.transpose(1, 0, 2), blocks)
    codes = lax.all_to_all(codes, "blocks", 0, 0, tiled=True)
    return exchange(position[pairs[0]], position[pairs[1]], codes, residues)


def solution(mesh):
    in_specs = (P("blocks", None, "parts"), P(), P())
    out_specs = P(None, ("parts", "blocks"), None)
    return jax.shard_map(shards, mesh=mesh, in_specs=in_specs, out_specs=out_specs, check_vma=False)
```

time: 262 us -> 233 us (0.89)
  Pallas kernels: 156 us -> 137 us
  local copies, waits for them, and re-layouts: 34.2 us -> 51.3 us
  blocking collectives: 15.1 us -> 0 us
  waiting for transfers between devices: 51.7 us -> 37 us
  starting transfers between devices: 4.52 us -> 7.43 us
    gather x2, local copies, waits for them, and re-layouts: 17.2 us -> 34.2 us  [shards(): return exchange(position[pairs[0]], position[pairs[1]], codes, residues)]
    pallas_call x1 -> x0, Pallas kernels: 16.7 us -> none  [featurize(): pl.pallas_call(feature_kernel, in_specs=[scalars, scalars, whole, whole],...]
    all_to_all x1 -> x0, blocking collectives: 15.1 us -> none  [shards(): meta = lax.all_to_all(meta, 'blocks', 0, 0, tiled=True)]
    all_to_all x1, waiting for transfers between devices: 51.7 us -> 37 us  [shards(): codes = lax.all_to_all(codes, 'blocks', 0, 0, tiled=True)]
    pallas_call x1, Pallas kernels: 135 us -> 131 us  [exchange(): pl.pallas_call(functools.partial(exchange_kernel, blocks, chunks), in_spe...]
    all_to_all x1, starting transfers between devices: 4.52 us -> 7.43 us  [shards(): codes = lax.all_to_all(codes, 'blocks', 0, 0, tiled=True)]
  transfers between devices with their start and end apart: 1 -> 1, of which waited for: 1 -> 1; matrix products, arithmetic and copies ran while one was open for 8% -> 16% of each run, Pallas kernels for 0% -> 0%
where the time goes in v2:
time: 233 us
  Pallas kernels  137 us (59%)
  local copies, waits for them, and re-layouts  51.3 us (22%)
  waiting for transfers between devices  37 us (16%)
  starting transfers between devices  7.43 us (3%)
    pallas_call x1, Pallas kernels, exchange(): pl.pallas_call(functools.partial(exchange_kernel, blocks, chunks), in_spe...  131 us
    all_to_all x1, waiting for transfers between devices, shards(): codes = lax.all_to_all(codes, 'blocks', 0, 0, tiled=True)  37 us
    gather x2, local copies, waits for them, and re-layouts, shards(): return exchange(position[pairs[0]], position[pairs[1]], codes, residues)  34.2 us
    unnamed x9, local copies, waits for them, and re-layouts  13 us
    all_to_all x1, starting transfers between devices, shards(): codes = lax.all_to_all(codes, 'blocks', 0, 0, tiled=True)  7.43 us
    pallas_call x1, Pallas kernels, encode(): pl.pallas_call(encode_kernel, grid=(blocks,), in_specs=[pl.BlockSpec((3,...  5.44 us
  transfers between devices with their start and end apart: 1, of which 1 were waited for; matrix products, arithmetic and copies ran while one was open for 16% of the time, Pallas kernels for 0%

profile of v2, /device:TPU:0, one launch (start us, length us, event | category | flops | bytes accessed | tf_op | source)
XLA Modules:
  0.0 232.7 jit_solution(15874912531823725483)
XLA Ops:
  0.0 0.0 copy-start.1
  0.0 3.2 %copy-done.1 = f32[40,3,16384]{2,0,1:T(8,128)S(1)} copy-done((f32[40,3,16384]{2,0,1:T(8,128)S(1)}, f32[40,3,16384]{2,0,1:T(8,128)}, u32[]{:S(2)}) %copy-start.1) | copy-done | bytes 7864344
  3.2 0.0 copy-start.3
  3.2 0.0 copy-start.2
  3.2 5.4 %shard_map.37 = s16[16,992,128]{2,1,0:T(8,128)(2,1)S(1)} custom-call(f32[3,40,16384]{2,1,0:T(8,128)S(1)} %bitcast.8), custom_call_target="tpu_custom_call" | custom-call | tf_op jit(solution)/shard_map/pallas_call | solution.py:57
  8.7 0.0 copy-start
  8.7 2.0 copy-done
  10.7 7.4 %all-to-all-start = ((s16[16,992,128]{2,1,0:T(8,128)(2,1)}), s16[16,992,128]{2,1,0:T(8,128)(2,1)}, u32[]{:S(2)}, u32[]{:S(2)}) async-start(s16[16,992,128]{2,1,0:T(8,128)(2,1)} %copy-done), calls=%async_computation | async-start | bytes 8126464 | tf_op jit(solution)/shard_map/all_to_all | solution.py:319
  18.1 0.0 copy-done.3
  18.1 4.1 %scatter_custom_fusion = s32[640]{0:T(1024)S(1)} fusion(s32[640]{0:T(1024)S(1)} %compare_select_fusion.2, s32[640]{0:T(1024)S(1)} %iota.3, s32[]{:T(128)} %constant.2.clone.1), kind=kCustom, calls=%fused_computation.8 | custom fusion | bytes 2564 | tf_op jit(solution)/shard_map/scatter | solution.py:316
  22.2 0.0 copy-done.2
  22.3 17.1 %gather_fusion.1 = s32[2048]{0:T(1024)} fusion(s32[640]{0:T(1024)S(1)} %scatter_custom_fusion, s32[2048]{0:T(1024)S(1)} %broadcast_clamp_fusion), kind=kCustom, calls=%fused_computation.1 | custom fusion | bytes 24576 | tf_op jit(solution)/shard_map/gather | solution.py:320
  39.4 17.1 %gather_fusion = s32[2048]{0:T(1024)} fusion(s32[640]{0:T(1024)S(1)} %scatter_custom_fusion, s32[2048]{0:T(1024)S(1)} %broadcast_clamp_fusion.1), kind=kCustom, calls=%fused_computation | custom fusion | bytes 24576 | tf_op jit(solution)/shard_map/gather | solution.py:320
  56.5 37.0 %all-to-all-done.code_ref = s16[16,992,128]{2,1,0:T(8,128)(2,1)} async-done(((s16[16,992,128]{2,1,0:T(8,128)(2,1)}), s16[16,992,128]{2,1,0:T(8,128)(2,1)}, u32[]{:S(2)}, u32[]{:S(2)}) %all-to-all-start) | async-done | bytes 4063264 | tf_op jit(solution)/shard_map/all_to_all | solution.py:319
  93.5 131.5 %shard_map.38 = bf16[4,1024,1024]{2,1,0:T(8,128)(2,1)} custom-call(s32[2048]{0:T(1024)} %gather_fusion, s32[2048]{0:T(1024)} %gather_fusion.1, s16[16,992,128]{2,1,0:T(8,128)(2,1)} %all-to-all-done.code_ref), custom_call_target="tpu_custom_call" | custom-call | tf_op jit(solution)/shard_map/pallas_call | solution.py:287
  225.0 7.8 %copy.5 = bf16[4,1024,1024]{2,1,0:T(8,128)(2,1)} copy(bf16[4,1024,1024]{2,1,0:T(8,128)(2,1)} %shard_map.38) | data formatting | bytes 16777216
  (5 shorter events, 0.0 us)
Async XLA Ops:
  0.0 3.2 %copy-start.1 = (f32[40,3,16384]{2,0,1:T(8,128)S(1)}, f32[40,3,16384]{2,0,1:T(8,128)}, u32[]{:S(2)}) copy-start(f32[40,3,16384]{2,0,1:T(8,128)} %param.3) | copy-start | bytes 23592964
  3.2 14.9 %copy-start.3 = (s32[640]{0:T(1024)S(1)}, s32[640]{0:T(1024)}, u32[]{:S(2)}) copy-start(s32[640]{0:T(1024)} %param.5) | copy-start | bytes 7684
  3.2 19.0 %copy-start.2 = (s32[2,2048]{1,0:T(2,128)S(1)}, s32[2,2048]{1,0:T(2,128)}, u32[]{:S(2)}) copy-start(s32[2,2048]{1,0:T(2,128)} %param.4) | copy-start | bytes 49156
  8.7 2.0 copy-start
  10.7 82.8 %all-to-all-start = ((s16[16,992,128]{2,1,0:T(8,128)(2,1)}), s16[16,992,128]{2,1,0:T(8,128)(2,1)}, u32[]{:S(2)}, u32[]{:S(2)}) async-start(s16[16,992,128]{2,1,0:T(8,128)(2,1)} %copy-done), calls=%async_computation | async-start | bytes 8126464 | tf_op jit(solution)/shard_map/all_to_all | solution.py:319

commit v3 on v2

--- a/solution.py
+++ b/solution.py
@@ -64,15 +64,15 @@
             pltpu.VMEM((res * rows, LANES), jnp.float32),
             pltpu.VMEM((4 * rows, LANES), jnp.float32),
         ],
-        compiler_params=pltpu.CompilerParams(vmem_limit_bytes=32 * 2**20),
+        compiler_params=pltpu.CompilerParams(vmem_limit_bytes=56 * 2**20),
     )(coords)
 
 
 PREV, SIDE, NEAR, FAR = range(4)
 
 
-def exchange_kernel(blocks, chunks, first_ref, second_ref, code_ref, out_ref, grid_ref, tmp, own_ref,
-                    own_t, visit, total, norms, own_norm, stage, send_sem, recv_sem, out_sem):
+def exchange_kernel(blocks, chunks, first_ref, second_ref, code_ref, out_ref, vis_out, own_out, grid_ref, tmp,
+                    own_ref, own_t, visit, total, norms, own_norm, send_sem, recv_sem, out_sem):
     me = lax.axis_index("blocks")
     core = me % 2
     side = (me // 2) % 2
@@ -230,40 +230,32 @@
 
     lax.fori_loop(0, chunks, arrive, 0)
 
-    slot_of = {PREV: 0, NEAR: 1, SIDE: 0, FAR: 1}
     round_of = {PREV: 3, SIDE: 1, NEAR: 2 - 2 * core, FAR: 2 * core}
 
-    def out_copy(stream):
-        return pltpu.make_async_copy(
-            stage.at[slot_of[stream]], out_ref.at[round_of[stream]], out_sem.at[stream]
+    def out_copies(stream):
+        at = round_of[stream]
+        return (
+            pltpu.make_async_copy(total.at[stream], out_ref.at[at], out_sem.at[2 * stream]),
+            pltpu.make_async_copy(norms.at[stream], vis_out.at[at], out_sem.at[2 * stream + 1]),
         )
 
     def finish(stream):
-        visiting = jnp.sum(norms[stream], axis=0, keepdims=True)
-
-        def rows_of(t, carry):
-            at = pl.ds(pl.multiple_of(t * tile, tile), tile)
-            shared = total[stream, at, :]
-            ratio = shared / (own_norm[at, :1] + visiting - shared + 1e-06)
-            stage[slot_of[stream], at, :] = (1.0 - ratio).astype(jnp.bfloat16)
-            return carry
-
-        lax.fori_loop(0, frames // tile, rows_of, 0)
-        out_copy(stream).start()
+        for each in out_copies(stream):
+            each.start()
 
     last = chunks // 2 - 1
+    finish(PREV)
+    finish(NEAR)
     own = jnp.sum(norms[4], axis=0, keepdims=True)
     own_norm[...] = jnp.broadcast_to(own, (LANES, frames)).T
-    finish(PREV)
+    own_copy = pltpu.make_async_copy(own_norm, own_out, out_sem.at[8])
+    own_copy.start()
     pass_far(chunks - 1)
-    finish(NEAR)
     add(SIDE, last)
-    out_copy(PREV).wait()
     finish(SIDE)
     copy(FAR, chunks - 2, prev, twin).wait_recv()
     copy(FAR, chunks - 1, prev, twin).wait_recv()
     add(FAR, last)
-    out_copy(NEAR).wait()
     finish(FAR)
 
     def drain(n, carry):
@@ -272,8 +264,10 @@
         return carry
 
     lax.fori_loop(0, chunks, drain, 0)
-    out_copy(SIDE).wait()
-    out_copy(FAR).wait()
+    own_copy.wait()
+    for stream in (PREV, NEAR, SIDE, FAR):
+        for each in out_copies(stream):
+            each.wait()
 
 
 def exchange(first, second, codes, residues):
@@ -287,8 +281,12 @@
     return pl.pallas_call(
         functools.partial(exchange_kernel, blocks, chunks),
         in_specs=[scalars, scalars, pl.BlockSpec(memory_space=pltpu.VMEM)],
-        out_specs=pl.BlockSpec(memory_space=pl.ANY),
-        out_shape=jax.ShapeDtypeStruct((ROUNDS, frames, frames), jnp.bfloat16),
+        out_specs=[pl.BlockSpec(memory_space=pl.ANY)] * 3,
+        out_shape=[
+            jax.ShapeDtypeStruct((ROUNDS, frames, frames), jnp.float32),
+            jax.ShapeDtypeStruct((ROUNDS, 8, frames), jnp.float32),
+            jax.ShapeDtypeStruct((frames, LANES), jnp.float32),
+        ],
         scratch_shapes=[
             pltpu.VMEM((3, residues, rows, LANES), jnp.float32),
             pltpu.VMEM((rows * 16, LANES), jnp.float32),
@@ -298,15 +296,39 @@
             pltpu.VMEM((4, frames, frames), jnp.float32),
             pltpu.VMEM((5, 8, frames), jnp.float32),
             pltpu.VMEM((frames, LANES), jnp.float32),
-            pltpu.VMEM((2, frames, frames), jnp.bfloat16),
             pltpu.SemaphoreType.DMA((4, chunks)),
             pltpu.SemaphoreType.DMA((4, chunks)),
-            pltpu.SemaphoreType.DMA((4,)),
+            pltpu.SemaphoreType.DMA((9,)),
         ],
         compiler_params=pltpu.CompilerParams(
             collective_id=1, has_side_effects=True, vmem_limit_bytes=60 * 2**20
         ),
     )(first, second, codes)
+
+
+def distance_kernel(shared_ref, visiting_ref, own_ref, out_ref):
+    visiting = jnp.sum(visiting_ref[0], axis=0, keepdims=True)
+    shared = shared_ref[0]
+    ratio = shared / (own_ref[:, :1] + visiting - shared + 1e-06)
+    out_ref[0] = (1.0 - ratio).astype(jnp.bfloat16)
+
+
+def distances_of(shared, visiting, own):
+    rounds, frames, _ = shared.shape
+    tile = min(256, frames)
+    block = pl.BlockSpec((1, tile, frames), lambda r, t: (r, t, 0))
+    return pl.pallas_call(
+        distance_kernel,
+        grid=(rounds, frames // tile),
+        in_specs=[
+            block,
+            pl.BlockSpec((1, 8, frames), lambda r, t: (r, 0, 0)),
+            pl.BlockSpec((tile, LANES), lambda r, t: (t, 0)),
+        ],
+        out_specs=block,
+        out_shape=jax.ShapeDtypeStruct(shared.shape, jnp.bfloat16),
+        compiler_params=pltpu.CompilerParams(vmem_limit_bytes=56 * 2**20),
+    )(shared, visiting, own)
 
 
 def shards(coords, pairs, res_slot):
@@ -317,7 +339,7 @@
     )
     codes = encode(coords.transpose(1, 0, 2), blocks)
     codes = lax.all_to_all(codes, "blocks", 0, 0, tiled=True)
-    return exchange(position[pairs[0]], position[pairs[1]], codes, residues)
+    return distances_of(*exchange(position[pairs[0]], position[pairs[1]], codes, residues))
 
 
 def solution(mesh):

time: 233 us -> 242 us (1.039)
  Pallas kernels: 137 us -> 158 us
  local copies, waits for them, and re-layouts: 51.3 us -> 38.3 us
    pallas_call x0 -> x1, Pallas kernels: none -> 16.5 us  [distances_of(): pl.pallas_call(distance_kernel, grid=(rounds, frames // tile), in_specs=[...]
    unnamed x9 -> x4, local copies, waits for them, and re-layouts: 13 us -> 0.01 us
    pallas_call x1, Pallas kernels: 5.44 us -> 12.9 us  [encode(): pl.pallas_call(encode_kernel, grid=(blocks,), in_specs=[pl.BlockSpec((3,...]
    pallas_call x1, Pallas kernels: 131 us -> 129 us  [exchange(): pl.pallas_call(functools.partial(exchange_kernel, blocks, chunks), in_spe...]
where the time goes in v3:
time: 242 us; the launch traced here: 241 us
  Pallas kernels  158 us (65%)
  local copies, waits for them, and re-layouts  38.3 us (16%)
  waiting for transfers between devices  37 us (15%)
  starting transfers between devices  7.43 us (3%)
    pallas_call x1, Pallas kernels, exchange(): pl.pallas_call(functools.partial(exchange_kernel, blocks, chunks), in_spe...  129 us
    all_to_all x1, waiting for transfers between devices, shards(): codes = lax.all_to_all(codes, 'blocks', 0, 0, tiled=True)  37 us
    gather x1, local copies, waits for them, and re-layouts, shards(): position[pairs[0]]  17.1 us
    gather x1, local copies, waits for them, and re-layouts, shards(): position[pairs[1]]  17.1 us
    pallas_call x1, Pallas kernels, distances_of(): pl.pallas_call(distance_kernel, grid=(rounds, frames // tile), in_specs=[...  16.5 us
    pallas_call x1, Pallas kernels, encode(): pl.pallas_call(encode_kernel, grid=(blocks,), in_specs=[pl.BlockSpec((3,...  12.9 us
    all_to_all x1, starting transfers between devices, shards(): codes = lax.all_to_all(codes, 'blocks', 0, 0, tiled=True)  7.43 us
  transfers between devices with their start and end apart: 1, of which 1 were waited for; matrix products, arithmetic and copies ran while one was open for 16% of the time, Pallas kernels for 0%

profile of v3, /device:TPU:0, one launch (start us, length us, event | category | flops | bytes accessed | tf_op | source)
XLA Modules:
  0.0 240.9 jit_solution(14574829828134273398)
XLA Ops:
  0.0 0.0 copy-start.1
  0.0 0.0 copy-start
  0.0 12.9 %shard_map.37 = s16[16,992,128]{2,1,0:T(8,128)(2,1)} custom-call(f32[3,40,16384]{2,1,0:T(8,128)} %bitcast.8), custom_call_target="tpu_custom_call" | custom-call | tf_op jit(solution)/shard_map/pallas_call | solution.py:57
  12.9 7.4 %all-to-all-start = ((s16[16,992,128]{2,1,0:T(8,128)(2,1)}), s16[16,992,128]{2,1,0:T(8,128)(2,1)}, u32[]{:S(2)}, u32[]{:S(2)}) async-start(s16[16,992,128]{2,1,0:T(8,128)(2,1)} %shard_map.37), calls=%async_computation | async-start | bytes 8126464 | tf_op jit(solution)/shard_map/all_to_all | solution.py:341
  20.4 0.0 copy-done.1
  20.4 4.1 %scatter_custom_fusion = s32[640]{0:T(1024)S(1)} fusion(s32[640]{0:T(1024)S(1)} %compare_select_fusion.2, s32[640]{0:T(1024)S(1)} %iota.3, s32[]{:T(128)} %constant.2.clone.1), kind=kCustom, calls=%fused_computation.8 | custom fusion | bytes 2564 | tf_op jit(solution)/shard_map/scatter | solution.py:338
  24.5 0.0 copy-done
  24.6 17.1 %gather_fusion.1 = s32[2048]{0:T(1024)} fusion(s32[640]{0:T(1024)S(1)} %scatter_custom_fusion, s32[2048]{0:T(1024)S(1)} %broadcast_clamp_fusion), kind=kCustom, calls=%fused_computation.1 | custom fusion | bytes 24576 | tf_op jit(solution)/shard_map/gather | solution.py:342
  41.6 17.1 %gather_fusion = s32[2048]{0:T(1024)} fusion(s32[640]{0:T(1024)S(1)} %scatter_custom_fusion, s32[2048]{0:T(1024)S(1)} %broadcast_clamp_fusion.1), kind=kCustom, calls=%fused_computation | custom fusion | bytes 24576 | tf_op jit(solution)/shard_map/gather | solution.py:342
  58.7 37.0 %all-to-all-done.code_ref = s16[16,992,128]{2,1,0:T(8,128)(2,1)} async-done(((s16[16,992,128]{2,1,0:T(8,128)(2,1)}), s16[16,992,128]{2,1,0:T(8,128)(2,1)}, u32[]{:S(2)}, u32[]{:S(2)}) %all-to-all-start) | async-done | bytes 4063264 | tf_op jit(solution)/shard_map/all_to_all | solution.py:341
  95.8 128.6 %shard_map.38 = (f32[4,1024,1024]{2,1,0:T(8,128)}, f32[4,8,1024]{2,1,0:T(8,128)}, f32[1024,128]{1,0:T(8,128)}) custom-call(s32[2048]{0:T(1024)} %gather_fusion, s32[2048]{0:T(1024)} %gather_fusion.1, s16[16,992,128]{2,1,0:T(8,128)(2,1)} %all-to-all-done.code_ref), custom_call_target="tpu_custom_call" | custom-call | tf_op jit(solution)/shard_map/pallas_call | solution.py:281
  224.4 16.5 %shard_map.39 = bf16[4,1024,1024]{2,1,0:T(8,128)(2,1)} custom-call(f32[4,1024,1024]{2,1,0:T(8,128)} %get-tuple-element.8.shared_ref, f32[4,8,1024]{2,1,0:T(8,128)} %get-tuple-element.9.visiting_ref, f32[1024,128]{1,0:T(8,128)} %get-tuple-element.10.own_ref), custom_call_target="tpu_custom_call" | custom-call | tf_op jit(solution)/shard_map/pallas_call | solution.py:320
  (5 shorter events, 0.0 us)
Async XLA Ops:
  0.0 20.4 %copy-start.1 = (s32[640]{0:T(1024)S(1)}, s32[640]{0:T(1024)}, u32[]{:S(2)}) copy-start(s32[640]{0:T(1024)} %param.5) | copy-start | bytes 7684
  0.0 24.5 %copy-start = (s32[2,2048]{1,0:T(2,128)S(1)}, s32[2,2048]{1,0:T(2,128)}, u32[]{:S(2)}) copy-start(s32[2,2048]{1,0:T(2,128)} %param.4) | copy-start | bytes 49156
  12.9 82.8 %all-to-all-start = ((s16[16,992,128]{2,1,0:T(8,128)(2,1)}), s16[16,992,128]{2,1,0:T(8,128)(2,1)}, u32[]{:S(2)}, u32[]{:S(2)}) async-start(s16[16,992,128]{2,1,0:T(8,128)(2,1)} %shard_map.37), calls=%async_computation | async-start | bytes 8126464 | tf_op jit(solution)/shard_map/all_to_all | solution.py:341
